TPU v7x, 32 devices: a whole 2x2x4 slice. The times are simulated.
32 devices in a mesh: gx: 8 (over z, x), gy: 4 (over y, core).
Axes of the slice: x: 2, y: 2, z: 4, core: 2. Of those that a mesh axis runs over, the one named last changes fastest.
Arguments:
- field: float32 [32, 64, 16, 384], P('gx', 'gy'), may hold values from -6 to 6
- inv_material: float32 [32, 64, 16], P('gx', 'gy'), may hold values from 0.5 to 2
- stiffness: bfloat16 [384, 384], replicated, may hold values from -0.15625 to 0.15625
- lift: bfloat16 [576, 384], replicated, may hold values from -1.25 to 1.25
- projection: bfloat16 [96, 64], replicated, may hold values from -0.625 to 0.625
- back_lift: bfloat16 [64, 384], replicated, may hold values from -0.75 to 0.75
- op_blocks: bfloat16 [8, 4, 64, 64], replicated, may hold values from -0.375 to 0.375
- op_columns: int32 [8, 4], replicated, may hold values from 0 to 7
- panel_dest: int32 [2048, 1], P(('gx', 'gy')), may hold values from 0 to 31; in each aligned block of 64 rows (0 to 63, 64 to 127, ...) at most 4 rows name the same one
- panel_anchor: int32 [2048], P(('gx', 'gy')), may hold values from 0 to 7
Outputs:
- advanced: float32 [32, 64, 16, 384], P('gx', 'gy')
Inputs may be any that keep to these rules, and one draw needn't show every extreme that they name: `panel_dest`: among the 64 panels of one device no brick is named more than 4 times; some device names one brick exactly 4 times.
All inputs are finite; a program needn't handle non-finite values.
Results may differ from a plain program's by a relative error of at most 0.0084.
Values may be sent and summed in bfloat16 or wider, within the bound.
A program may use at most 128 MiB of HBM per device.

v0:
```python
import functools

import jax
import jax.numpy as jnp
import numpy as np
from jax import lax
from jax.experimental import pallas as pl
from jax.experimental.pallas import tpu as pltpu
from jax.sharding import PartitionSpec as P

NBLK = 8
STEP = 0.25
F32 = jnp.float32
BF16 = jnp.bfloat16
MESH = pl.DeviceIdType.MESH


def selectors():
    nodes = np.arange(384).reshape(6, 4, 4, 4)
    faces = (
        nodes[:, 0], nodes[:, 3], nodes[:, :, 0], nodes[:, :, 3], nodes[..., 0], nodes[..., 3],
    )
    sel = np.zeros((384, 768), np.float32)
    for f, face in enumerate(faces):
        sel[face.reshape(-1), 128 * f + np.arange(96)] = 1
    return sel


def dot(a, b):
    return jnp.dot(a, b, preferred_element_type=F32)


def kernel(
    nx, ny, field, inv, stiff, lift, proj, back_lift, ops, col_code, send_code, recv_code, sel, out,
    tot, acc, sb, yz, xhi, xlo, yhi_send, ylo_send, x_low, x_high, y_low, y_high, lift_pad, top_w,
    back_w, op_w, place_send, place_recv, grid_mask, a_send, a_recv, b_send, b_recv, stack, top,
    a_ssem, a_rsem, b_ssem, b_rsem, h_ssem, h_rsem,
):
    n = nx * ny
    gx, gy = lax.axis_index("gx"), lax.axis_index("gy")
    ex_n, ez_n = 4, 16
    per = field.shape[0] // ex_n
    rows = per * ez_n

    def peer(i):
        return (lax.rem(gx + i // ny, nx), lax.rem(gy + lax.rem(i, ny), ny))

    barrier = pltpu.get_barrier_semaphore()

    @pl.loop(1, n)
    def _(i):
        pl.semaphore_signal(barrier, inc=1, device_id=peer(i), device_id_type=MESH)

    lift_pad[...] = jnp.zeros_like(lift_pad)
    for f in range(6):
        lift_pad[128 * f : 128 * f + 96, :] = lift[96 * f : 96 * f + 96, :]
    lane64 = lax.broadcasted_iota(jnp.int32, (64, 128), 1)
    row64 = lax.broadcasted_iota(jnp.int32, (64, 128), 0)
    to_left = (lane64 == row64).astype(F32).astype(BF16)
    to_right = (lane64 == row64 + 64).astype(F32).astype(BF16)
    source = dot(sel[:, 640:736], proj[...]).astype(BF16)
    top_w[:, 0:128] = dot(source, to_left).astype(BF16)
    top_w[:, 128:256] = dot(source, to_right).astype(BF16)
    back_w[...] = jnp.zeros_like(back_w)
    back_w[0:64, :] = back_lift[...]
    back_w[192:256, :] = back_lift[...]
    for q in range(NBLK // 2):
        for r in range(4):
            block = (
                dot(ops[2 * q, r], to_left) + dot(ops[2 * q + 1, r], to_right)
            ).astype(BF16)
            op_w[128 * r : 128 * r + 64, 128 * q : 128 * q + 128] = block
            op_w[128 * r + 64 : 128 * r + 128, 128 * q : 128 * q + 128] = block
    place_send[...] = jnp.where(
        lax.broadcasted_iota(jnp.int32, (4 * n, 128), 0) == send_code[...], 1.0, 0.0
    ).astype(BF16)
    place_recv[...] = jnp.where(
        lax.broadcasted_iota(jnp.int32, (128, 4 * n), 1) == recv_code[...], 1.0, 0.0
    ).astype(BF16)
    half = lax.broadcasted_iota(jnp.int32, (32, 128), 1) // 64
    for q in range(4):
        grid_mask[q] = jnp.where(col_code[...] == 2 * q + half, 1.0, 0.0)
    diagonal = jnp.where(
        lax.broadcasted_iota(jnp.int32, (NBLK, 512), 1) // 64
        == lax.broadcasted_iota(jnp.int32, (NBLK, 512), 0),
        1.0,
        0.0,
    )
    tot[...] = jnp.zeros_like(tot)
    acc[...] = jnp.zeros_like(acc)
    top[...] = field[:, ez_n - 1, :]

    @pl.when(gx == 0)
    def _():
        x_low[...] = jnp.zeros_like(x_low)

    @pl.when(gx == nx - 1)
    def _():
        x_high[...] = jnp.zeros_like(x_high)

    @pl.when(gy == 0)
    def _():
        y_low[...] = jnp.zeros_like(y_low)

    @pl.when(gy == ny - 1)
    def _():
        y_high[...] = jnp.zeros_like(y_high)

    pl.semaphore_wait(barrier, n - 1)

    z_at = lax.rem(lax.broadcasted_iota(jnp.int32, (rows, 128), 0), ez_n)
    not_first = jnp.where(z_at == 0, 0.0, 1.0)
    not_last = jnp.where(z_at == ez_n - 1, 0.0, 1.0)

    @pl.loop(0, 4)
    def _(s):
        c = jnp.where(s == 0, 0.0, jnp.where(s == 3, STEP, STEP / 2)).astype(F32)
        b = jnp.where(s == 0, 0.0, jnp.where(s == 1, 1.0, 2.0)).astype(F32)

        def halo(k, src, dst, dx, dy):
            return pltpu.make_async_remote_copy(
                src_ref=src, dst_ref=dst.at[s], send_sem=h_ssem.at[k], recv_sem=h_rsem.at[k, s],
                device_id=(gx + dx, gy + dy), device_id_type=MESH,
            )

        halos = (
            (halo(0, xhi.at[4], x_low, 1, 0), gx < nx - 1, gx > 0),
            (halo(1, xlo.at[0], x_high, -1, 0), gx > 0, gx < nx - 1),
            (halo(2, yhi_send, y_low, 0, 1), gy < ny - 1, gy > 0),
            (halo(3, ylo_send, y_high, 0, -1), gy > 0, gy < ny - 1),
        )

        pair = dot(top[...].astype(BF16), top_w[...])
        both = jnp.concatenate([pair[:, 0:128], pair[:, 128:256]], axis=0).astype(BF16)
        sums = dot(place_send[...], both)
        for j in range(n):
            a_send[j] = sums[4 * j : 4 * j + 4, :]

        def a_copy(i):
            return pltpu.make_async_remote_copy(
                src_ref=a_send.at[i], dst_ref=a_recv.at[s, i], send_sem=a_ssem,
                recv_sem=a_rsem.at[s], device_id=peer(i), device_id_type=MESH,
            )

        @pl.loop(1, n)
        def _(i):
            a_copy(i).start()

        @pl.loop(0, ex_n)
        def _(ex):
            at = pl.ds(ex * per, per)
            k = [
                tot[at, :, 128 * t : 128 * t + 128] * inv[at]
                for t in range(3)
            ]
            k = jnp.concatenate(k, axis=2)
            acc[at] = acc[at] + b * k
            sec = (field[at] + c * k).astype(BF16)
            sb[at] = sec
            flat = sec.reshape(rows, 384)
            x_both = dot(flat, sel[:, 0:256]).astype(BF16)
            xlo[ex] = x_both[:, 0:128]
            xhi[ex + 1] = x_both[:, 128:256]
            y_both = dot(flat, sel[:, 256:512]).astype(BF16)
            yz[ex, :, 0:256] = y_both
            ylo_send[ex] = y_both[0:16, 0:128]
            yhi_send[ex] = y_both[rows - 16 : rows, 128:256]
            yz[ex, :, 256:512] = dot(flat, sel[:, 512:768]).astype(BF16)

        for copy, sends, _r in halos:
            pl.when(sends)(copy.start)

        @pl.loop(0, ex_n)
        def _(ex):
            at = pl.ds(ex * per, per)
            zlo = yz[ex, :, 256:384].astype(F32)
            zhi = yz[ex, :, 384:512].astype(F32)
            below = pltpu.roll(zhi, 1, 0) * not_first
            above = pltpu.roll(zlo, rows - 1, 0) * not_last
            jump = jnp.concatenate(
                [(below - zlo).astype(BF16), (above - zhi).astype(BF16)], axis=1
            )
            got = dot(sb[at].reshape(rows, 384), stiff[...]) + dot(jump, lift_pad[512:768, :])
            tot[at] = got.reshape(per, ez_n, 384)

        a_all = a_recv.at[s, pl.ds(1, n - 1)]
        pltpu.make_async_copy(a_all, a_all, a_rsem.at[s]).wait()
        grid = a_send[0]
        for j in range(1, n):
            grid = grid + a_recv[s, j]
        grid = grid.astype(BF16).astype(F32)
        picked = grid_mask[0] * grid[0:1]
        for q in range(1, 4):
            picked = picked + grid_mask[q] * grid[q : q + 1]
        wide = jnp.concatenate([picked[8 * r : 8 * r + 8] for r in range(4)], axis=1)
        fields = jnp.sum(dot(wide.astype(BF16), op_w[...]) * diagonal, axis=0, keepdims=True)
        fields = fields.astype(BF16).astype(F32)
        for q in range(4):
            b_send[q : q + 1, :] = fields[:, 128 * q : 128 * q + 128]

        def b_copy(i):
            return pltpu.make_async_remote_copy(
                src_ref=b_send, dst_ref=b_recv.at[s, i], send_sem=b_ssem,
                recv_sem=b_rsem.at[s], device_id=peer(i), device_id_type=MESH,
            )

        @pl.loop(1, n)
        def _(i):
            b_copy(i).start()

        for copy, _s, receives in halos:
            pl.when(receives)(copy.wait_recv)
        for copy, sends, _r in halos:
            pl.when(sends)(copy.wait_send)
        xhi[0] = x_low[s]
        xlo[4] = x_high[s]

        @pl.loop(0, ex_n)
        def _(ex):
            at = pl.ds(ex * per, per)
            own_lo, own_hi = xlo[ex].astype(F32), xhi[ex + 1].astype(F32)
            jump_x = jnp.concatenate(
                [
                    (xhi[ex].astype(F32) - own_lo).astype(BF16),
                    (xlo[ex + 1].astype(F32) - own_hi).astype(BF16),
                ],
                axis=1,
            )
            ylo, yhi = yz[ex, :, 0:128].astype(F32), yz[ex, :, 128:256].astype(F32)
            low = jnp.concatenate([y_low[s, ex].astype(F32), yhi[0 : rows - 16]], axis=0)
            high = jnp.concatenate([ylo[16:rows], y_high[s, ex].astype(F32)], axis=0)
            jump_y = jnp.concatenate([(low - ylo).astype(BF16), (high - yhi).astype(BF16)], axis=1)
            got = dot(jump_x, lift_pad[0:256, :]) + dot(jump_y, lift_pad[256:512, :])
            tot[at] = tot[at] + got.reshape(per, ez_n, 384)

        b_all = b_recv.at[s, pl.ds(1, n - 1)]
        pltpu.make_async_copy(b_all, b_all, b_rsem.at[s]).wait()
        stack[0:4, :] = b_send[...]
        for j in range(1, n):
            stack[4 * j : 4 * j + 4, :] = b_recv[s, j]
        at_panels = dot(place_recv[...], stack[...].astype(BF16)).astype(BF16)
        at_panels = jnp.concatenate([at_panels[0:64], at_panels[64:128]], axis=1)
        top_tot = tot[:, ez_n - 1, :] + dot(at_panels, back_w[...])
        tot[:, ez_n - 1, :] = top_tot
        inv_top = inv[:, ez_n - 1, :]
        c_next = jnp.where(s == 2, STEP, STEP / 2).astype(F32)
        top[...] = field[:, ez_n - 1, :] + c_next * (
            jnp.concatenate([inv_top, inv_top, inv_top], axis=1) * top_tot
        )
        a_out = a_send.at[pl.ds(1, n - 1)]
        pltpu.make_async_copy(a_out, a_out, a_ssem).wait()
        pltpu.make_async_copy(b_all, b_all, b_ssem).wait()

    @pl.loop(0, ex_n)
    def _(ex):
        at = pl.ds(ex * per, per)
        for t in range(3):
            lanes = slice(128 * t, 128 * t + 128)
            out[at, :, lanes] = field[at, :, lanes] + (STEP / 6) * (
                acc[at, :, lanes] + tot[at, :, lanes] * inv[at]
            )


def body(
    nx, ny, field, inv_material, stiffness, lift, projection, back_lift, op_blocks, op_columns,
    panel_dest, panel_anchor,
):
    ex_n, ey_n, ez_n = field.shape[:3]
    panels, n = ex_n * ey_n, nx * ny
    rows = ey_n * ez_n
    gx, gy = lax.axis_index("gx"), lax.axis_index("gy")
    dest = panel_dest[:, 0]
    dx, dy = dest // ny, dest % ny
    pair, odd = panel_anchor // 2, panel_anchor % 2
    ahead = ((dx - gx + nx) % nx * ny + (dy - gy + ny) % ny) * 4 + pair
    behind = ((gx - dx + nx) % nx * ny + (gy - dy + ny) % ny) * 4 + pair
    send_code = jnp.stack([jnp.where(odd == p, ahead, -1) for p in (0, 1)]).reshape(1, 128)
    recv_code = jnp.stack([jnp.where(odd == p, behind, -1) for p in (0, 1)]).reshape(128, 1)
    col_code = op_columns.T.reshape(32, 1)
    inv = jnp.broadcast_to(inv_material[..., None], (ex_n, ey_n, ez_n, 128))
    vmem = pl.BlockSpec(memory_space=pltpu.VMEM)
    out = pl.pallas_call(
        functools.partial(kernel, nx, ny),
        out_shape=jax.ShapeDtypeStruct((panels, ez_n, 384), F32),
        in_specs=[vmem] * 11,
        out_specs=vmem,
        scratch_shapes=[
            pltpu.VMEM((panels, ez_n, 384), F32),
            pltpu.VMEM((panels, ez_n, 384), F32),
            pltpu.VMEM((panels, ez_n, 384), BF16),
            pltpu.VMEM((ex_n, rows, 512), BF16),
            pltpu.VMEM((ex_n + 1, rows, 128), BF16),
            pltpu.VMEM((ex_n + 1, rows, 128), BF16),
            pltpu.VMEM((ex_n, 16, 128), BF16),
            pltpu.VMEM((ex_n, 16, 128), BF16),
            pltpu.VMEM((4, rows, 128), BF16),
            pltpu.VMEM((4, rows, 128), BF16),
            pltpu.VMEM((4, ex_n, 16, 128), BF16),
            pltpu.VMEM((4, ex_n, 16, 128), BF16),
            pltpu.VMEM((768, 384), BF16),
            pltpu.VMEM((384, 256), BF16),
            pltpu.VMEM((256, 384), BF16),
            pltpu.VMEM((512, 512), BF16),
            pltpu.VMEM((4 * n, 128), BF16),
            pltpu.VMEM((128, 4 * n), BF16),
            pltpu.VMEM((4, 32, 128), F32),
            pltpu.VMEM((n, 4, 128), F32),
            pltpu.VMEM((4, n, 4, 128), F32),
            pltpu.VMEM((4, 128), F32),
            pltpu.VMEM((4, n, 4, 128), F32),
            pltpu.VMEM((4 * n, 128), F32),
            pltpu.VMEM((panels, 384), F32),
            pltpu.SemaphoreType.DMA,
            pltpu.SemaphoreType.DMA((4,)),
            pltpu.SemaphoreType.DMA,
            pltpu.SemaphoreType.DMA((4,)),
            pltpu.SemaphoreType.DMA((4,)),
            pltpu.SemaphoreType.DMA((4, 4)),
        ],
        compiler_params=pltpu.CompilerParams(
            collective_id=0, has_side_effects=True, vmem_limit_bytes=48 * 2**20
        ),
    )(
        field.reshape(panels, ez_n, 384), inv.reshape(panels, ez_n, 128), stiffness, lift,
        projection, back_lift, op_blocks, col_code, send_code, recv_code,
        jnp.asarray(selectors(), BF16),
    )
    return out.reshape(ex_n, ey_n, ez_n, 384)


def solution(mesh):
    return jax.shard_map(
        functools.partial(body, mesh.shape["gx"], mesh.shape["gy"]),
        mesh=mesh,
        in_specs=(
            P("gx", "gy", None, None),
            P("gx", "gy", None),
            P(),
            P(),
            P(),
            P(),
            P(),
            P(),
            P(("gx", "gy"), None),
            P(("gx", "gy")),
        ),
        out_specs=P("gx", "gy", None, None),
        check_vma=False,
    )
```

profile of v0, /device:TPU:0, one launch (start us, length us, event | category | flops | bytes accessed | tf_op | source)
XLA Modules:
  0.0 60.8 jit_solution(8396547555590058465)
XLA Ops:
  0.0 0.7 %fusion.3 = (s32[1,64]{1,0:T(1,128)S(1)}, s32[64]{0:T(128)S(1)}, s32[64]{0:T(128)S(1)}, s32[64]{0:T(128)S(1)}, s32[64]{0:T(128)S(1)}) fusion(s32[64,1]{0,1:T(1,128)} %param.19, s32[]{:T(128)S(6)} %axis_index.25, s32[]{:T(128)S(6)} %axis_index.23, s32[64]{0:T(128)} %param.20), kind=kLoop, calls=%fused_computation.31 | loop fusion | flops 4480 | bytes 1800 | tf_op jit(solution)/shard_map/stack | solution.py:278
  0.7 0.7 %fusion.2 = (s32[1,64]{1,0:T(1,128)S(1)}, s32[64]{0:T(128)S(1)}) fusion(s32[64]{0:T(128)S(1)} %get-tuple-element.7, s32[64]{0:T(128)S(1)} %get-tuple-element.9, s32[]{:T(128)S(6)} %axis_index.25, s32[64,1]{0,1:T(1,128)} %param.19, s32[64]{0:T(128)S(1)} %get-tuple-element.8, s32[]{:T(128)S(6)} %axis_index.23), kind=kLoop, calls=%fused_computation.30 | loop fusion | flops 2752 | bytes 1544 | tf_op jit(solution)/shard_map/stack | solution.py:277
  1.4 0.1 reshape.21.send_code
  1.5 0.8 %reshape.24.col_code = s32[32,1]{1,0:T(8,128)S(1)} reshape(s32[4,8]{1,0:T(4,128)} %bitcast.35) | data formatting | bytes 256 | tf_op jit(solution)/shard_map/reshape | solution.py:279
  2.2 0.8 %copy.12.proj = bf16[96,64]{1,0:T(8,128)(2,1)S(1)} copy(bf16[96,64]{0,1:T(8,128)(2,1)} %param.15) | data formatting | bytes 24576 | tf_op args[4]
  3.1 0.1 reshape.25.recv_code
  3.2 0.9 %broadcast_in_dim.14.inv = f32[64,16,128]{2,1,0:T(8,128)S(1)} broadcast(f32[64,16]{1,0:T(8,128)} %bitcast.34), dimensions={0,1} | broadcast | bytes 528384 | tf_op jit(solution)/shard_map/broadcast_in_dim | solution.py:280
  4.2 0.0 copy-start
  4.2 1.4 %copy-done = f32[4,16,16,384]{3,2,1,0:T(8,128)S(1)} copy-done((f32[4,16,16,384]{3,2,1,0:T(8,128)S(1)}, f32[4,16,16,384]{3,2,1,0:T(8,128)}, u32[]{:S(2)}) %copy-start) | copy-done | bytes 1572888
  5.6 0.0 copy-start.1
  5.6 1.1 %copy-done.1 = bf16[384,768]{1,0:T(8,128)(2,1)S(1)} copy-done((bf16[384,768]{1,0:T(8,128)(2,1)S(1)}, bf16[384,768]{1,0:T(8,128)(2,1)}, u32[]{:S(2)}) %copy-start.1) | copy-done | bytes 589848
  6.7 0.0 copy-start.2
  6.7 1.0 %copy-done.2 = bf16[8,4,64,64]{3,2,1,0:T(8,128)(2,1)S(1)} copy-done((bf16[8,4,64,64]{3,2,1,0:T(8,128)(2,1)S(1)}, bf16[8,4,64,64]{3,2,1,0:T(8,128)(2,1)}, u32[]{:S(2)}) %copy-start.2) | copy-done | bytes 262168
  7.7 0.0 copy-start.3
  7.7 1.0 %copy-done.3 = bf16[576,384]{1,0:T(8,128)(2,1)S(1)} copy-done((bf16[576,384]{1,0:T(8,128)(2,1)S(1)}, bf16[576,384]{1,0:T(8,128)(2,1)}, u32[]{:S(2)}) %copy-start.3) | copy-done | bytes 442392
  8.7 0.0 copy-start.4
  8.7 1.0 %copy-done.4 = bf16[384,384]{1,0:T(8,128)(2,1)S(1)} copy-done((bf16[384,384]{1,0:T(8,128)(2,1)S(1)}, bf16[384,384]{1,0:T(8,128)(2,1)}, u32[]{:S(2)}) %copy-start.4) | copy-done | bytes 294936
  9.7 0.0 copy-start.5
  9.7 0.8 %copy-done.5 = bf16[64,384]{1,0:T(8,128)(2,1)S(1)} copy-done((bf16[64,384]{1,0:T(8,128)(2,1)S(1)}, bf16[64,384]{1,0:T(8,128)(2,1)}, u32[]{:S(2)}) %copy-start.5) | copy-done | bytes 49176
  10.5 49.1 %shard_map.109 = f32[64,16,384]{2,1,0:T(8,128)S(1)} custom-call(f32[64,16,384]{2,1,0:T(8,128)S(1)} %bitcast.33, f32[64,16,128]{2,1,0:T(8,128)S(1)} %broadcast_in_dim.14.inv, bf16[384,384]{1,0:T(8,128)(2,1)S(1)} %copy-done.4, bf16[576,384]{1,0:T(8,128)(2,1)S(1)} %copy-done.3, bf16[96,64]{1,0:T(8,128)(2,1)S(1)} %copy.12.proj, bf16[64,384]{1,0:T(8,128)(2,1)S(1)} %copy-done.5, ...), custom_call_target="tpu_custom_call" | custom-call | tf_op jit(solution)/shard_map/pallas_call | solution.py:282
  59.6 1.1 %copy.16 = f32[4,16,16,384]{3,2,1,0:T(8,128)} copy(f32[4,16,16,384]{3,2,1,0:T(8,128)S(1)} %bitcast.32) | data formatting | bytes 3145728
  (2 shorter events, 0.0 us)
Async XLA Ops:
  4.2 1.4 %copy-start = (f32[4,16,16,384]{3,2,1,0:T(8,128)S(1)}, f32[4,16,16,384]{3,2,1,0:T(8,128)}, u32[]{:S(2)}) copy-start(f32[4,16,16,384]{3,2,1,0:T(8,128)} %param.11) | copy-start | bytes 4718596
  5.6 1.1 %copy-start.1 = (bf16[384,768]{1,0:T(8,128)(2,1)S(1)}, bf16[384,768]{1,0:T(8,128)(2,1)}, u32[]{:S(2)}) copy-start(bf16[384,768]{1,0:T(8,128)(2,1)} %constant.87.clone.sel) | copy-start | bytes 1769476
  6.7 1.0 %copy-start.2 = (bf16[8,4,64,64]{3,2,1,0:T(8,128)(2,1)S(1)}, bf16[8,4,64,64]{3,2,1,0:T(8,128)(2,1)}, u32[]{:S(2)}) copy-start(bf16[8,4,64,64]{3,2,1,0:T(8,128)(2,1)} %ops.1) | copy-start | bytes 786436
  7.7 1.0 %copy-start.3 = (bf16[576,384]{1,0:T(8,128)(2,1)S(1)}, bf16[576,384]{1,0:T(8,128)(2,1)}, u32[]{:S(2)}) copy-start(bf16[576,384]{1,0:T(8,128)(2,1)} %lift.1) | copy-start | bytes 1327108
  8.7 1.0 %copy-start.4 = (bf16[384,384]{1,0:T(8,128)(2,1)S(1)}, bf16[384,384]{1,0:T(8,128)(2,1)}, u32[]{:S(2)}) copy-start(bf16[384,384]{1,0:T(8,128)(2,1)} %stiff.1) | copy-start | bytes 884740
  9.7 0.8 %copy-start.5 = (bf16[64,384]{1,0:T(8,128)(2,1)S(1)}, bf16[64,384]{1,0:T(8,128)(2,1)}, u32[]{:S(2)}) copy-start(bf16[64,384]{1,0:T(8,128)(2,1)} %back_lift.1) | copy-start | bytes 147460
where the time goes:
time: 61.3 us; the launch traced here: 60.8 us
  Pallas kernels  49.1 us (80%)
  local copies, waits for them, and re-layouts  10.2 us (17%)
  other arithmetic  1.39 us (2%)
    pallas_call x1, Pallas kernels, body(): pl.pallas_call(functools.partial(kernel, nx, ny), out_shape=jax.ShapeDtyp...  49.1 us
    unnamed x14, local copies, waits for them, and re-layouts  8.24 us

commit v1 on v0

--- a/solution.py
+++ b/solution.py
@@ -31,15 +31,29 @@
 
 
 def kernel(
-    nx, ny, field, inv, stiff, lift, proj, back_lift, ops, col_code, send_code, recv_code, sel, out,
-    tot, acc, sb, yz, xhi, xlo, yhi_send, ylo_send, x_low, x_high, y_low, y_high, lift_pad, top_w,
-    back_w, op_w, place_send, place_recv, grid_mask, a_send, a_recv, b_send, b_recv, stack, top,
+    nx, ny, field_in, inv_in, stiff_in, lift_in, proj_in, back_in, ops_in, columns_in, dest_in,
+    anchor_in, sel_in, out, field, inv_raw, stiff, lift, proj, back_lift, ops, columns, dest, anchor,
+    sel, load_sem, inv, tot, acc, yz, xhi, xlo, yhi_send, ylo_send, x_low, x_high, y_low, y_high, lift_pad, top_w,
+    back_w, op_w, place_send, place_recv, grid_mask, a_send, a_recv, b_send, b_recv, stack,
+    first_send, first_recv, grid_sum, weight, reflect,
     a_ssem, a_rsem, b_ssem, b_rsem, h_ssem, h_rsem,
 ):
     n = nx * ny
     gx, gy = lax.axis_index("gx"), lax.axis_index("gy")
     ex_n, ez_n = 4, 16
     per = field.shape[0] // ex_n
+    loads = [
+        pltpu.make_async_copy(src, dst, load_sem.at[i])
+        for i, (src, dst) in enumerate(
+            (
+                (columns_in, columns), (dest_in, dest), (anchor_in, anchor), (proj_in, proj),
+                (sel_in, sel), (ops_in, ops), (back_in, back_lift), (lift_in, lift),
+                (inv_in, inv_raw), (field_in, field), (stiff_in, stiff),
+            )
+        )
+    ]
+    for load in loads:
+        load.start()
     rows = per * ez_n
 
     def peer(i):
@@ -51,6 +65,10 @@
     def _(i):
         pl.semaphore_signal(barrier, inc=1, device_id=peer(i), device_id_type=MESH)
 
+    for load in loads:
+        load.wait()
+
+    inv[...] = jnp.broadcast_to(inv_raw[...][:, :, None], inv.shape)
     lift_pad[...] = jnp.zeros_like(lift_pad)
     for f in range(6):
         lift_pad[128 * f : 128 * f + 96, :] = lift[96 * f : 96 * f + 96, :]
@@ -58,37 +76,87 @@
     row64 = lax.broadcasted_iota(jnp.int32, (64, 128), 0)
     to_left = (lane64 == row64).astype(F32).astype(BF16)
     to_right = (lane64 == row64 + 64).astype(F32).astype(BF16)
-    source = dot(sel[:, 640:736], proj[...]).astype(BF16)
+    source = lax.dot_general(
+        sel[:, 640:736], proj[...], (((1,), (1,)), ((), ())), preferred_element_type=F32
+    ).astype(BF16)
     top_w[:, 0:128] = dot(source, to_left).astype(BF16)
     top_w[:, 128:256] = dot(source, to_right).astype(BF16)
     back_w[...] = jnp.zeros_like(back_w)
     back_w[0:64, :] = back_lift[...]
     back_w[192:256, :] = back_lift[...]
     for q in range(NBLK // 2):
+        block = dot(ops[2 * q].reshape(256, 64), to_left) + dot(
+            ops[2 * q + 1].reshape(256, 64), to_right
+        )
+        block = block.astype(BF16)
+        lanes = slice(128 * q, 128 * q + 128)
         for r in range(4):
-            block = (
-                dot(ops[2 * q, r], to_left) + dot(ops[2 * q + 1, r], to_right)
-            ).astype(BF16)
-            op_w[128 * r : 128 * r + 64, 128 * q : 128 * q + 128] = block
-            op_w[128 * r + 64 : 128 * r + 128, 128 * q : 128 * q + 128] = block
+            piece = block[64 * r : 64 * r + 64]
+            op_w[128 * r : 128 * r + 64, lanes] = piece
+            op_w[128 * r + 64 : 128 * r + 128, lanes] = piece
+
+    def codes(where, block, axis):
+        dx, dy = where // ny, lax.rem(where, ny)
+        pair, odd = block // 2, lax.rem(block, 2)
+        if axis == 1:
+            there = lax.rem(dx - gx + nx, nx) * ny + lax.rem(dy - gy + ny, ny)
+        else:
+            there = lax.rem(gx - dx + nx, nx) * ny + lax.rem(gy - dy + ny, ny)
+        code = there * 4 + pair
+        return jnp.concatenate([jnp.where(odd == p, code, -1) for p in (0, 1)], axis=axis)
+
+    def column(row):
+        size = row.shape[1]
+        eye = lax.broadcasted_iota(jnp.int32, (size, size), 0) == lax.broadcasted_iota(
+            jnp.int32, (size, size), 1
+        )
+        picked = jnp.where(eye, row.astype(F32), 0.0)
+        return jnp.sum(picked, axis=1, keepdims=True).astype(jnp.int32)
+
+    send_code = codes(dest[...], anchor[...], 1)
+    recv_code = codes(column(dest[...]), column(anchor[...]), 0)
     place_send[...] = jnp.where(
-        lax.broadcasted_iota(jnp.int32, (4 * n, 128), 0) == send_code[...], 1.0, 0.0
+        lax.broadcasted_iota(jnp.int32, (4 * n, 128), 0) == send_code, 1.0, 0.0
     ).astype(BF16)
     place_recv[...] = jnp.where(
-        lax.broadcasted_iota(jnp.int32, (128, 4 * n), 1) == recv_code[...], 1.0, 0.0
+        lax.broadcasted_iota(jnp.int32, (128, 4 * n), 1) == recv_code, 1.0, 0.0
     ).astype(BF16)
-    half = lax.broadcasted_iota(jnp.int32, (32, 128), 1) // 64
-    for q in range(4):
-        grid_mask[q] = jnp.where(col_code[...] == 2 * q + half, 1.0, 0.0)
+    half = lax.broadcasted_iota(jnp.int32, (8, 128), 1) // 64
+    for r in range(4):
+        named = column(columns[r : r + 1, :])
+        for q in range(4):
+            grid_mask[q, 8 * r : 8 * r + 8] = jnp.where(named == 2 * q + half, 1.0, 0.0)
     diagonal = jnp.where(
         lax.broadcasted_iota(jnp.int32, (NBLK, 512), 1) // 64
         == lax.broadcasted_iota(jnp.int32, (NBLK, 512), 0),
         1.0,
         0.0,
     )
+    echo = dot(back_lift[...], top_w[:, 0:128]).astype(BF16)
+    reflect[...] = jnp.zeros_like(reflect)
+    reflect[0:64, :] = echo
+    reflect[64:128, :] = dot(back_lift[...], top_w[:, 128:256]).astype(BF16)
+    b_send[...] = jnp.zeros_like(b_send)
     tot[...] = jnp.zeros_like(tot)
     acc[...] = jnp.zeros_like(acc)
-    top[...] = field[:, ez_n - 1, :]
+    inv_top = inv[:, ez_n - 1, :]
+    left = lax.broadcasted_iota(jnp.int32, inv_top.shape, 1) < 64
+    shares = jnp.concatenate(
+        [jnp.where(left, inv_top, 0.0), jnp.where(left, 0.0, inv_top)], axis=0
+    )
+    coarse = shares.astype(BF16)
+    fine = (shares - coarse.astype(F32)).astype(BF16)
+    weights = dot(place_send[...], coarse) + dot(place_send[...], fine)
+
+    def panel_sums(section):
+        pair = dot(section.astype(BF16), top_w[...])
+        both = jnp.concatenate([pair[:, 0:128], pair[:, 128:256]], axis=0).astype(BF16)
+        return dot(place_send[...], both)
+
+    sums = panel_sums(field[:, ez_n - 1, :])
+    for j in range(n):
+        first_send[j, 0:4] = sums[4 * j : 4 * j + 4, :]
+        first_send[j, 4:8] = weights[4 * j : 4 * j + 4, :]
 
     @pl.when(gx == 0)
     def _():
@@ -107,6 +175,16 @@
         y_high[...] = jnp.zeros_like(y_high)
 
     pl.semaphore_wait(barrier, n - 1)
+
+    def first_copy(i):
+        return pltpu.make_async_remote_copy(
+            src_ref=first_send.at[i], dst_ref=first_recv.at[i], send_sem=a_ssem,
+            recv_sem=a_rsem.at[0], device_id=peer(i), device_id_type=MESH,
+        )
+
+    @pl.loop(1, n)
+    def _(i):
+        first_copy(i).start()
 
     z_at = lax.rem(lax.broadcasted_iota(jnp.int32, (rows, 128), 0), ez_n)
     not_first = jnp.where(z_at == 0, 0.0, 1.0)
@@ -130,24 +208,9 @@
             (halo(3, ylo_send, y_high, 0, -1), gy > 0, gy < ny - 1),
         )
 
-        pair = dot(top[...].astype(BF16), top_w[...])
-        both = jnp.concatenate([pair[:, 0:128], pair[:, 128:256]], axis=0).astype(BF16)
-        sums = dot(place_send[...], both)
-        for j in range(n):
-            a_send[j] = sums[4 * j : 4 * j + 4, :]
-
-        def a_copy(i):
-            return pltpu.make_async_remote_copy(
-                src_ref=a_send.at[i], dst_ref=a_recv.at[s, i], send_sem=a_ssem,
-                recv_sem=a_rsem.at[s], device_id=peer(i), device_id_type=MESH,
-            )
-
-        @pl.loop(1, n)
-        def _(i):
-            a_copy(i).start()
-
         @pl.loop(0, ex_n)
-        def _(ex):
+        def _(turn):
+            ex = lax.rem(turn + ex_n - 1, ex_n)
             at = pl.ds(ex * per, per)
             k = [
                 tot[at, :, 128 * t : 128 * t + 128] * inv[at]
@@ -156,39 +219,63 @@
             k = jnp.concatenate(k, axis=2)
             acc[at] = acc[at] + b * k
             sec = (field[at] + c * k).astype(BF16)
-            sb[at] = sec
             flat = sec.reshape(rows, 384)
             x_both = dot(flat, sel[:, 0:256]).astype(BF16)
             xlo[ex] = x_both[:, 0:128]
             xhi[ex + 1] = x_both[:, 128:256]
             y_both = dot(flat, sel[:, 256:512]).astype(BF16)
-            yz[ex, :, 0:256] = y_both
+            yz[ex] = y_both
             ylo_send[ex] = y_both[0:16, 0:128]
             yhi_send[ex] = y_both[rows - 16 : rows, 128:256]
-            yz[ex, :, 256:512] = dot(flat, sel[:, 512:768]).astype(BF16)
-
-        for copy, sends, _r in halos:
-            pl.when(sends)(copy.start)
-
-        @pl.loop(0, ex_n)
-        def _(ex):
-            at = pl.ds(ex * per, per)
-            zlo = yz[ex, :, 256:384].astype(F32)
-            zhi = yz[ex, :, 384:512].astype(F32)
+            for at_turn in range(2):
+                copy, sends, _r = halos[at_turn]
+                pl.when(jnp.logical_and(sends, turn == at_turn))(copy.start)
+            z_both = dot(flat, sel[:, 512:768])
+            zlo = z_both[:, 0:128]
+            zhi = z_both[:, 128:256]
             below = pltpu.roll(zhi, 1, 0) * not_first
             above = pltpu.roll(zlo, rows - 1, 0) * not_last
             jump = jnp.concatenate(
                 [(below - zlo).astype(BF16), (above - zhi).astype(BF16)], axis=1
             )
-            got = dot(sb[at].reshape(rows, 384), stiff[...]) + dot(jump, lift_pad[512:768, :])
+            got = dot(flat, stiff[...]) + dot(jump, lift_pad[512:768, :])
             tot[at] = got.reshape(per, ez_n, 384)
 
-        a_all = a_recv.at[s, pl.ds(1, n - 1)]
-        pltpu.make_async_copy(a_all, a_all, a_rsem.at[s]).wait()
-        grid = a_send[0]
-        for j in range(1, n):
-            grid = grid + a_recv[s, j]
-        grid = grid.astype(BF16).astype(F32)
+        for copy, sends, _r in halos[2:]:
+            pl.when(sends)(copy.start)
+
+        a_out = a_send.at[pl.ds(1, n - 1)]
+
+        @pl.when(s == 0)
+        def _():
+            came = first_recv.at[pl.ds(1, n - 1)]
+            pltpu.make_async_copy(came, came, a_rsem.at[0]).wait()
+            pltpu.make_async_copy(came, came, a_ssem).wait()
+            total = first_send[0]
+            for j in range(1, n):
+                total = total + first_recv[j]
+            grid_sum[...] = total[0:4]
+            weight[...] = total[4:8]
+
+        @pl.when(s > 0)
+        def _():
+            a_all = a_recv.at[s, pl.ds(1, n - 1)]
+            pltpu.make_async_copy(a_all, a_all, a_rsem.at[s]).wait()
+            pltpu.make_async_copy(a_out, a_out, a_ssem).wait()
+            total = a_send[0]
+            for j in range(1, n):
+                total = total + a_recv[s, j]
+            fed = b_send[...].astype(BF16)
+            back = jnp.concatenate(
+                [
+                    dot(fed[:, 0:64], reflect[0:64, :])[:, 0:64],
+                    dot(fed[:, 64:128], reflect[64:128, :])[:, 64:128],
+                ],
+                axis=1,
+            )
+            grid_sum[...] = total + c * weight[...] * back
+
+        grid = grid_sum[...].astype(BF16).astype(F32)
         picked = grid_mask[0] * grid[0:1]
         for q in range(1, 4):
             picked = picked + grid_mask[q] * grid[q : q + 1]
@@ -233,6 +320,26 @@
             got = dot(jump_x, lift_pad[0:256, :]) + dot(jump_y, lift_pad[256:512, :])
             tot[at] = tot[at] + got.reshape(per, ez_n, 384)
 
+        c_next = jnp.where(s == 2, STEP, STEP / 2).astype(F32)
+
+        def a_copy(i):
+            return pltpu.make_async_remote_copy(
+                src_ref=a_send.at[i], dst_ref=a_recv.at[s + 1, i], send_sem=a_ssem,
+                recv_sem=a_rsem.at[s + 1], device_id=peer(i), device_id_type=MESH,
+            )
+
+        @pl.when(s < 3)
+        def _():
+            inv_top = inv[:, ez_n - 1, :]
+            inv_top = jnp.concatenate([inv_top, inv_top, inv_top], axis=1)
+            sums = panel_sums(field[:, ez_n - 1, :] + c_next * (inv_top * tot[:, ez_n - 1, :]))
+            for j in range(n):
+                a_send[j] = sums[4 * j : 4 * j + 4, :]
+
+            @pl.loop(1, n)
+            def _(i):
+                a_copy(i).start()
+
         b_all = b_recv.at[s, pl.ds(1, n - 1)]
         pltpu.make_async_copy(b_all, b_all, b_rsem.at[s]).wait()
         stack[0:4, :] = b_send[...]
@@ -240,15 +347,7 @@
             stack[4 * j : 4 * j + 4, :] = b_recv[s, j]
         at_panels = dot(place_recv[...], stack[...].astype(BF16)).astype(BF16)
         at_panels = jnp.concatenate([at_panels[0:64], at_panels[64:128]], axis=1)
-        top_tot = tot[:, ez_n - 1, :] + dot(at_panels, back_w[...])
-        tot[:, ez_n - 1, :] = top_tot
-        inv_top = inv[:, ez_n - 1, :]
-        c_next = jnp.where(s == 2, STEP, STEP / 2).astype(F32)
-        top[...] = field[:, ez_n - 1, :] + c_next * (
-            jnp.concatenate([inv_top, inv_top, inv_top], axis=1) * top_tot
-        )
-        a_out = a_send.at[pl.ds(1, n - 1)]
-        pltpu.make_async_copy(a_out, a_out, a_ssem).wait()
+        tot[:, ez_n - 1, :] = tot[:, ez_n - 1, :] + dot(at_panels, back_w[...])
         pltpu.make_async_copy(b_all, b_all, b_ssem).wait()
 
     @pl.loop(0, ex_n)
@@ -268,27 +367,30 @@
     ex_n, ey_n, ez_n = field.shape[:3]
     panels, n = ex_n * ey_n, nx * ny
     rows = ey_n * ez_n
-    gx, gy = lax.axis_index("gx"), lax.axis_index("gy")
-    dest = panel_dest[:, 0]
-    dx, dy = dest // ny, dest % ny
-    pair, odd = panel_anchor // 2, panel_anchor % 2
-    ahead = ((dx - gx + nx) % nx * ny + (dy - gy + ny) % ny) * 4 + pair
-    behind = ((gx - dx + nx) % nx * ny + (gy - dy + ny) % ny) * 4 + pair
-    send_code = jnp.stack([jnp.where(odd == p, ahead, -1) for p in (0, 1)]).reshape(1, 128)
-    recv_code = jnp.stack([jnp.where(odd == p, behind, -1) for p in (0, 1)]).reshape(128, 1)
-    col_code = op_columns.T.reshape(32, 1)
-    inv = jnp.broadcast_to(inv_material[..., None], (ex_n, ey_n, ez_n, 128))
+    hbm = pl.BlockSpec(memory_space=pltpu.HBM)
     vmem = pl.BlockSpec(memory_space=pltpu.VMEM)
     out = pl.pallas_call(
         functools.partial(kernel, nx, ny),
         out_shape=jax.ShapeDtypeStruct((panels, ez_n, 384), F32),
-        in_specs=[vmem] * 11,
+        in_specs=[hbm] * 11,
         out_specs=vmem,
         scratch_shapes=[
             pltpu.VMEM((panels, ez_n, 384), F32),
+            pltpu.VMEM((panels, ez_n), F32),
+            pltpu.VMEM(stiffness.shape, BF16),
+            pltpu.VMEM(lift.shape, BF16),
+            pltpu.VMEM(projection.shape[::-1], BF16),
+            pltpu.VMEM(back_lift.shape, BF16),
+            pltpu.VMEM(op_blocks.shape, BF16),
+            pltpu.VMEM(op_columns.shape[::-1], jnp.int32),
+            pltpu.VMEM((1, panels), jnp.int32),
+            pltpu.VMEM((1, panels), jnp.int32),
+            pltpu.VMEM((384, 768), BF16),
+            pltpu.SemaphoreType.DMA((11,)),
+            pltpu.VMEM((panels, ez_n, 128), F32),
             pltpu.VMEM((panels, ez_n, 384), F32),
-            pltpu.VMEM((panels, ez_n, 384), BF16),
-            pltpu.VMEM((ex_n, rows, 512), BF16),
+            pltpu.VMEM((panels, ez_n, 384), F32),
+            pltpu.VMEM((ex_n, rows, 256), BF16),
             pltpu.VMEM((ex_n + 1, rows, 128), BF16),
             pltpu.VMEM((ex_n + 1, rows, 128), BF16),
             pltpu.VMEM((ex_n, 16, 128), BF16),
@@ -309,7 +411,11 @@
             pltpu.VMEM((4, 128), F32),
             pltpu.VMEM((4, n, 4, 128), F32),
             pltpu.VMEM((4 * n, 128), F32),
-            pltpu.VMEM((panels, 384), F32),
+            pltpu.VMEM((n, 8, 128), F32),
+            pltpu.VMEM((n, 8, 128), F32),
+            pltpu.VMEM((4, 128), F32),
+            pltpu.VMEM((4, 128), F32),
+            pltpu.VMEM((128, 128), BF16),
             pltpu.SemaphoreType.DMA,
             pltpu.SemaphoreType.DMA((4,)),
             pltpu.SemaphoreType.DMA,
@@ -318,11 +424,12 @@
             pltpu.SemaphoreType.DMA((4, 4)),
         ],
         compiler_params=pltpu.CompilerParams(
-            collective_id=0, has_side_effects=True, vmem_limit_bytes=48 * 2**20
+            collective_id=0, has_side_effects=True, vmem_limit_bytes=60 * 2**20
         ),
     )(
-        field.reshape(panels, ez_n, 384), inv.reshape(panels, ez_n, 128), stiffness, lift,
-        projection, back_lift, op_blocks, col_code, send_code, recv_code,
+        field.reshape(panels, ez_n, 384), inv_material.reshape(panels, ez_n), stiffness, lift,
+        projection.T, back_lift, op_blocks, op_columns.T, panel_dest.reshape(1, panels),
+        panel_anchor.reshape(1, panels),
         jnp.asarray(selectors(), BF16),
     )
     return out.reshape(ex_n, ey_n, ez_n, 384)

time: 61.3 us -> 50 us (0.82)
  local copies, waits for them, and re-layouts: 10.2 us -> 2.67 us
  Pallas kernels: 49.1 us -> 47.2 us
  other arithmetic: 1.39 us -> 0 us
    unnamed x14 -> x1, local copies, waits for them, and re-layouts: 8.24 us -> 2.67 us
    pallas_call x1, Pallas kernels: 49.1 us -> 47.2 us  [body(): pl.pallas_call(functools.partial(kernel, nx, ny), out_shape=jax.ShapeDtyp...]
    another operation x4 -> x0, other arithmetic: 1.39 us -> none  [the longest x2 0.7 us: body(): jnp.stack([jnp.where(odd == p, behind, -1) for p in (0, 1)]).reshape(128, 1)]
    reshape x3 -> x0, local copies, waits for them, and re-layouts: 0.98 us -> none  [the longest x1 0.76 us: body(): col_code = op_columns.T.reshape(32, 1)]
    broadcast_in_dim x1 -> x0, local copies, waits for them, and re-layouts: 0.95 us -> none  [body(): inv = jnp.broadcast_to(inv_material[..., None], (ex_n, ey_n, ez_n, 128))]
where the time goes in v1:
time: 50 us; the launch traced here: 49.9 us
  Pallas kernels  47.2 us (94%)
  local copies, waits for them, and re-layouts  2.67 us (5%)
    pallas_call x1, Pallas kernels, body(): pl.pallas_call(functools.partial(kernel, nx, ny), out_shape=jax.ShapeDtyp...  47.2 us
    unnamed x1, local copies, waits for them, and re-layouts  2.67 us

profile of v1, /device:TPU:0, one launch (start us, length us, event | category | flops | bytes accessed | tf_op | source)
XLA Modules:
  0.0 49.9 jit_solution(4457555233096764374)
XLA Ops:
  0.0 47.2 %shard_map.109 = f32[64,16,384]{2,1,0:T(8,128)} custom-call(f32[64,16,384]{2,1,0:T(8,128)} %bitcast.8, f32[64,16]{1,0:T(8,128)} %bitcast.9, bf16[384,384]{1,0:T(8,128)(2,1)} %stiff_in.1, bf16[576,384]{1,0:T(8,128)(2,1)} %lift_in.1, bf16[64,96]{1,0:T(8,128)(2,1)} %bitcast.10, bf16[64,384]{1,0:T(8,128)(2,1)} %back_in.1, bf16[8,4,64,64]{3,2,1,0:T(8,128)(2,1)} %ops_in.1, ...), custom_call_target="tpu_custom_call" | custom-call | tf_op jit(solution)/shard_map/pallas_call | solution.py:372
  47.2 2.7 %copy.13 = f32[4,16,16,384]{3,2,1,0:T(8,128)} copy(f32[4,16,16,384]{3,2,1,0:T(8,128)} %bitcast.7) | data formatting | bytes 3145728
